TPU v7x, 32 devices: a whole 2x2x4 slice. The times are simulated.
32 devices in a mesh: space: 8 (over y, x, core), snap: 4 (over z).
Axes of the slice: x: 2, y: 2, z: 4, core: 2. Of those that a mesh axis runs over, the one named last changes fastest.
Arguments:
- snapshots: bfloat16 [8192, 2048], P('space', 'snap'), may hold values from -6 to 6
- eigen_vectors: bfloat16 [2048, 512], replicated, may hold values from -0.125 to 0.125
- singular: float32 [512], replicated, as said below
Outputs:
- pod_modes: bfloat16 [8192, 512], P(('space', 'snap'))
- reduced_operator: float32 [512, 512], replicated
Inputs may be any that keep to these rules, and one draw needn't show every extreme that they name: `singular`: every entry lies between a third of and three times the fourth root of 8192.
All inputs are finite; a program needn't handle non-finite values.
Results may differ from a plain program's by a relative error of at most 0.002.
Values may be sent and summed in bfloat16 or wider, within the bound.
A program may use at most 64 MiB of HBM per device.

v0:
```python
import jax
import jax.numpy as jnp
from jax import lax
from jax.sharding import PartitionSpec as P


def shifted(block, axis, distance):
    devices = range(lax.axis_size(axis))
    route = [((i - distance) % len(devices), i) for i in devices]
    return lax.ppermute(block, axis, route)


def per_device(snapshots, eigen_vectors, singular):
    columns = snapshots.shape[1]
    following = shifted(snapshots[:, :1], "snap", -1)
    advanced = jnp.concatenate([snapshots[:, 1:], following], axis=1)
    offset = lax.axis_index("snap") * columns
    vector_rows = lax.dynamic_slice_in_dim(eigen_vectors, offset, columns, 0)
    first = jnp.dot(snapshots, vector_rows, preferred_element_type=jnp.float32)
    second = jnp.dot(advanced, vector_rows, preferred_element_type=jnp.float32)
    summed = lax.psum_scatter(
        jnp.concatenate([first, second], axis=1), "snap", scatter_dimension=0, tiled=True
    )
    width = eigen_vectors.shape[1]
    projected = summed[:, :width]
    forward = summed[:, width:]
    pod_modes = (projected / singular[None, :]).astype(jnp.bfloat16)
    pushed = (forward / singular[None, :]).astype(jnp.bfloat16)
    local_term = lax.dot_general(
        pod_modes, pushed, (((0,), (0,)), ((), ())), preferred_element_type=jnp.float32
    )
    reduced_operator = lax.psum(local_term, ("space", "snap"))
    return (pod_modes, reduced_operator)


def solution(mesh):
    in_specs = (P("space", "snap"), P(), P())
    out_specs = (P(("space", "snap"), None), P())
    return jax.shard_map(
        per_device, mesh=mesh, in_specs=in_specs, out_specs=out_specs, check_vma=False
    )
```

profile of v0, /device:TPU:1, one launch (start us, length us, event | category | flops | bytes accessed | tf_op | source)
XLA Modules:
  0.0 246.6 jit_solution(11202204177687018445)
XLA Ops:
  7.2 0.0 copy-start
  7.2 0.0 copy-start.1
  7.2 0.0 reduce-scatter.2.cloned.1.call-start
  7.2 1.8 slice.13
  9.1 4.2 %collective-permute-start = (bf16[1024,1]{1,0:T(8,128)(2,1)}, bf16[1024,1]{1,0:T(8,128)(2,1)S(1)}, u32[]{:S(2)}, u32[]{:S(2)}) collective-permute-start(bf16[1024,1]{1,0:T(8,128)(2,1)} %slice.13), channel_id=1, source_target_pairs={{1,0},{2,1},{3,2},{0,3},{5,4},{6,5},{7,6},{4,7},{9,8},{10,9},{11,1... | collective-permute-start | bytes 6152 | tf_op jit(solution)/shard_map/ppermute | solution.py:10
  13.2 0.0 copy-done
  13.2 2.0 convolution_bitcast_fusion
  15.2 0.0 copy-done.1
  15.2 0.5 slice.12
  15.7 2.8 %collective-permute-done = bf16[1024,1]{1,0:T(8,128)(2,1)S(1)} collective-permute-done((bf16[1024,1]{1,0:T(8,128)(2,1)}, bf16[1024,1]{1,0:T(8,128)(2,1)S(1)}, u32[]{:S(2)}, u32[]{:S(2)}) %collective-permute-start) | collective-permute-done | bytes 2080 | tf_op jit(solution)/shard_map/ppermute | solution.py:10
  18.5 0.8 fusion
  19.3 2.5 %pad_maximum_fusion = f32[1024,1024]{0,1:T(8,128)} fusion(f32[1024,512]{0,1:T(8,128)S(1)} %fusion, f32[1024,512]{0,1:T(8,128)S(1)} %convolution_bitcast_fusion), kind=kLoop, calls=%fused_computation | loop fusion | flops 1048576 | bytes 8388608 | tf_op jit(solution)/shard_map/concatenate | solution.py:22
  21.7 0.0 copy-start.2
  21.7 0.0 reduce-scatter.2.cloned.1.call-update
  21.8 0.0 all-reduce.2.cloned.1.call-start
  21.8 79.6 %reduce-scatter.2.cloned.1.call-done = f32[256,1024]{0,1:T(8,128)} async-done(((f32[1024,1024]{0,1:T(8,128)}), f32[256,1024]{0,1:T(8,128)}) %reduce-scatter.2.cloned.1.call-update) | async-done | bytes 1048592 | tf_op jit(solution)/shard_map/reduce_scatter | solution.py:21
  101.4 0.0 copy-done.2
  101.4 1.2 fusion.5
  102.6 2.4 fusion.8
  105.0 0.0 all-reduce.2.cloned.1.call-update
  105.0 0.8 copy.5
  105.9 131.6 %all-reduce.2.cloned.1.call-done = f32[512,512]{1,0:T(8,128)} async-done(((f32[512,512]{1,0:T(8,128)}), f32[512,512]{1,0:T(8,128)}) %all-reduce.2.cloned.1.call-update) | async-done | bytes 1048592 | tf_op jit(solution)/shard_map/psum | solution.py:32
  237.5 2.3 copy.7
Async XLA Ops:
  7.2 6.0 %copy-start = (bf16[2048,512]{1,0:T(8,128)(2,1)S(1)}, bf16[2048,512]{1,0:T(8,128)(2,1)}, u32[]{:S(2)}) copy-start(bf16[2048,512]{1,0:T(8,128)(2,1)} %param.4) | copy-start | bytes 6291460
  7.2 8.0 %copy-start.1 = (bf16[1024,512]{1,0:T(8,128)(2,1)S(1)}, bf16[1024,512]{1,0:T(8,128)(2,1)}, u32[]{:S(2)}) copy-start(bf16[1024,512]{1,0:T(8,128)(2,1)} %param.3) | copy-start | bytes 3145732
  7.2 94.2 %reduce-scatter.2.cloned.1.call-start = ((), (), s32[]{:S(2)}) async-start(), calls=%async_computation.1 | async-start | bytes 5242880 | tf_op jit(solution)/shard_map/reduce_scatter | solution.py:21
  9.1 9.4 %collective-permute-start = (bf16[1024,1]{1,0:T(8,128)(2,1)}, bf16[1024,1]{1,0:T(8,128)(2,1)S(1)}, u32[]{:S(2)}, u32[]{:S(2)}) collective-permute-start(bf16[1024,1]{1,0:T(8,128)(2,1)} %slice.13), channel_id=1, source_target_pairs={{1,0},{2,1},{3,2},{0,3},{5,4},{6,5},{7,6},{4,7},{9,8},{10,9},{11,1... | collective-permute-start | bytes 6152 | tf_op jit(solution)/shard_map/ppermute | solution.py:10
  21.7 79.7 %copy-start.2 = (f32[512]{0:T(512)S(1)}, f32[512]{0:T(512)}, u32[]{:S(2)}) copy-start(f32[512]{0:T(512)} %param.5) | copy-start | bytes 6148
  21.8 215.7 %all-reduce.2.cloned.1.call-start = ((), (), s32[]{:S(2)}) async-start(), calls=%async_computation.2 | async-start | bytes 2097152 | tf_op jit(solution)/shard_map/psum | solution.py:32
Sparse Core Ops, SparseCore 0:
  21.9 79.4 reduce-scatter.1
  108.0 129.4 all-reduce.1
where the time goes:
time: 248 us; the launch traced here: 247 us
  waiting for transfers between devices  214 us (86%)
  between operations  14.1 us (6%)
  local copies, waits for them, and re-layouts  5.41 us (2%)
  matrix products  5.17 us (2%)
  starting transfers between devices  4.23 us (2%)
  other arithmetic  3.64 us (1%)
    psum x1, waiting for transfers between devices, per_device(): reduced_operator = lax.psum(local_term, ('space', 'snap'))  132 us
    reduce_scatter x1, waiting for transfers between devices, per_device(): lax.psum_scatter(jnp.concatenate([first, second], axis=1), 'snap', scatte...  79.6 us
  transfers between devices with their start and end apart: 3, of which 3 were waited for; matrix products, arithmetic and copies ran while one was open for 1% of the time, Pallas kernels for 0%

commit v1 on v0

v1 whole, which is shorter than its diff:
```python
import functools

import jax
import jax.numpy as jnp
from jax import lax
from jax.experimental import pallas as pl
from jax.experimental.pallas import tpu as pltpu
from jax.sharding import PartitionSpec as P

MESH = pl.DeviceIdType.MESH
F32, BF16 = jnp.float32, jnp.bfloat16
PLANE = 8


def shift_vectors(vectors, snaps, rank):
    rows = 64

    def one(i, above):
        at = pl.ds(pl.multiple_of(i * rows, rows), rows)
        chunk = vectors[at, :rank].astype(F32)
        moved = pltpu.roll(chunk, 1, 0)
        first = lax.broadcasted_iota(jnp.int32, chunk.shape, 0) == 0
        vectors[at, rank:] = jnp.where(first, above, moved).astype(BF16)
        return chunk[rows - 1 :, :]

    last = vectors[snaps - 16 :, :rank].astype(F32)[15:, :]
    lax.fori_loop(0, snaps // rows, one, last)


def kernel(sizes, x_hbm, e_hbm, s_ref, modes_hbm, op_hbm, *scratch):
    n_space, n_snap, groups, fused = sizes
    (xbuf, vectors, modes, e_sem, x_send, x_recv, own_sem, m_sem) = scratch[:8]
    space, snap = lax.axis_index("space"), lax.axis_index("snap")
    rows, rank = modes.shape
    cols = x_hbm.shape[1]
    snaps = cols * n_snap
    piece = rows // groups

    load_e = pltpu.make_async_copy(e_hbm, vectors.at[:, :rank], e_sem)
    load_e.start()
    own = pltpu.make_async_copy(
        x_hbm.at[pl.ds(pl.multiple_of(snap * rows, rows), rows), :],
        xbuf.at[:, pl.ds(pl.multiple_of(snap * cols, cols), cols)],
        own_sem,
    )
    own.start()

    barrier = pltpu.get_barrier_semaphore()
    for j in range(1, n_snap):
        pl.semaphore_signal(
            barrier, inc=1, device_id=(space, lax.rem(snap + j, n_snap)), device_id_type=MESH
        )
    if fused:
        for j in range(1, n_space):
            pl.semaphore_signal(
                barrier, inc=1, device_id=(lax.rem(space + j, n_space), snap), device_id_type=MESH
            )
    pl.semaphore_wait(barrier, n_snap - 1 + (n_space - 1 if fused else 0))

    def block_copy(g, j):
        to = lax.rem(snap + j, n_snap)
        return pltpu.make_async_remote_copy(
            src_ref=x_hbm.at[pl.ds(pl.multiple_of(to * rows + g * piece, piece), piece), :],
            dst_ref=xbuf.at[
                pl.ds(pl.multiple_of(g * piece, piece), piece),
                pl.ds(pl.multiple_of(snap * cols, cols), cols),
            ],
            send_sem=x_send.at[g, j],
            recv_sem=x_recv.at[g, j],
            device_id=(space, to),
            device_id_type=MESH,
        )

    order = sorted(range(1, n_snap), key=lambda j: -min(j, n_snap - j))

    def send_blocks(g, _):
        for j in order:
            block_copy(g, j).start()
        return _

    lax.fori_loop(0, groups, send_blocks, 0)

    load_e.wait()
    shift_vectors(vectors, snaps, rank)
    own.wait()

    def project(g):
        at = pl.ds(pl.multiple_of(g * piece, piece), piece)
        for j in order:
            block_copy(g, j).wait_recv()
        sums = jnp.dot(xbuf[at, :], vectors[...], preferred_element_type=F32)
        scale = s_ref[...]
        mode = (sums[:, :rank] / scale).astype(BF16)
        push = (sums[:, rank:] / scale).astype(BF16)
        modes[at, :] = mode
        pltpu.make_async_copy(modes.at[at, :], modes_hbm.at[at, :], m_sem.at[g]).start()
        return mode, push

    def finish(g, _):
        at = pl.ds(pl.multiple_of(g * piece, piece), piece)
        for j in order:
            block_copy(g, j).wait_send()
        pltpu.make_async_copy(modes.at[at, :], modes_hbm.at[at, :], m_sem.at[g]).wait()
        return _

    contract = (((0,), (0,)), ((), ()))
    if not fused:
        (pushed, op, op_sem) = scratch[8:]

        def step(g, _):
            at = pl.ds(pl.multiple_of(g * piece, piece), piece)
            pushed[at, :] = project(g)[1]
            return _

        lax.fori_loop(0, groups, step, 0)
        op[...] = lax.dot_general(modes[...], pushed[...], contract, preferred_element_type=F32)
        out = pltpu.make_async_copy(op, op_hbm, op_sem)
        out.start()
        lax.fori_loop(0, groups, finish, 0)
        out.wait()
        return

    (stage, gathered, term, parts, whole, p_send, p_recv, p_own,
     r_send, r_recv, z_send, z_recv, w_send, f_send, w_recv, op_sem) = scratch[8:]
    tall, wide = rank // 4, rank // 2

    def share_copy(g, j):
        to = lax.rem(space + j, n_space)
        return pltpu.make_async_remote_copy(
            src_ref=stage.at[g, to],
            dst_ref=gathered.at[g, pl.ds(pl.multiple_of(space * piece, piece), piece), :],
            send_sem=p_send.at[g, j],
            recv_sem=p_recv.at[g, j],
            device_id=(to, snap),
            device_id_type=MESH,
        )

    def share_own(g):
        return pltpu.make_async_copy(
            stage.at[g, space],
            gathered.at[g, pl.ds(pl.multiple_of(space * piece, piece), piece), :],
            p_own.at[g],
        )

    def add_term(g):
        share_own(g).wait()
        for j in range(1, n_space):
            share_copy(g, j).wait_recv()
        return lax.dot_general(
            gathered[g, :, :tall], gathered[g, :, tall:], contract, preferred_element_type=F32
        )

    def step(g, _):
        mode, push = project(g)
        for p in range(n_space):
            stage[g, p, :, :tall] = mode[:, (p // 2) * tall : (p // 2 + 1) * tall]
            stage[g, p, :, tall:] = push[:, (p % 2) * wide : (p % 2 + 1) * wide]
        for j in (3, 4, 5, 2, 6, 1, 7):
            share_copy(g, j).start()
        share_own(g).start()

        @pl.when(g > 0)
        def _add():
            term[...] += add_term(g - 1)

        return _

    term[...] = jnp.zeros_like(term)
    lax.fori_loop(0, groups, step, 0)
    term[...] += add_term(groups - 1)

    slab = tall // n_snap

    def reduce_copy(j):
        to = lax.rem(snap + j, n_snap)
        return pltpu.make_async_remote_copy(
            src_ref=term.at[pl.ds(pl.multiple_of(to * slab, slab), slab), :],
            dst_ref=parts.at[j],
            send_sem=r_send.at[j],
            recv_sem=r_recv.at[j],
            device_id=(space, to),
            device_id_type=MESH,
        )

    for j in order:
        reduce_copy(j).start()
    mine = pl.multiple_of(snap * slab, slab)
    total = term[pl.ds(mine, slab), :]
    for j in order:
        reduce_copy(j).wait_recv()
    for j in order:
        total = total + parts[j]

    def place(p, start, size):
        return whole.at[
            pl.ds(pl.multiple_of((p // 2) * tall + start, size), size),
            pl.ds(pl.multiple_of(lax.rem(p, 2) * wide, wide), wide),
        ]

    parts[0] = total
    piece_at = place(space, mine, slab)
    piece_at[...] = parts[0].astype(BF16)

    def slab_copy(j):
        return pltpu.make_async_remote_copy(
            src_ref=piece_at,
            dst_ref=piece_at,
            send_sem=z_send.at[j],
            recv_sem=z_recv.at[j],
            device_id=(space, lax.rem(snap + j, n_snap)),
            device_id_type=MESH,
        )

    def slab_arrival(j):
        origin = lax.rem(snap + n_snap - j, n_snap)
        at = place(space, origin * slab, slab)
        return pltpu.make_async_remote_copy(
            src_ref=at, dst_ref=at, send_sem=z_send.at[j], recv_sem=z_recv.at[j],
            device_id=(space, lax.rem(snap + j, n_snap)), device_id_type=MESH,
        )

    for j in order:
        slab_copy(j).start()
    for j in order:
        slab_arrival(j).wait_recv()

    chip, core = space // 2, lax.rem(space, 2)
    chips = n_space // 2
    sibling = space + 1 - 2 * core

    def spread(p, to, send_sem):
        return pltpu.make_async_remote_copy(
            src_ref=place(p, 0, tall), dst_ref=place(p, 0, tall),
            send_sem=send_sem, recv_sem=w_recv.at[p],
            device_id=(to, snap), device_id_type=MESH,
        )

    def partner(j):
        return lax.rem(chip + j, chips) * 2 + core

    for j in (2, 1, 3):
        spread(space, partner(j), w_send.at[j]).start()
    spread(space, sibling, f_send.at[0]).start()
    for j in (1, 3, 2):
        came = partner(j)
        spread(came, sibling, f_send.at[j]).wait_recv()
        spread(came, sibling, f_send.at[j]).start()
    for j in range(chips):
        there = lax.rem(chip + j, chips) * 2 + 1 - core
        spread(there, sibling, f_send.at[j]).wait_recv()
    out = pltpu.make_async_copy(whole, op_hbm, op_sem)
    out.start()

    lax.fori_loop(0, groups, finish, 0)

    def finish_shares(g, _):
        for j in range(1, n_space):
            share_copy(g, j).wait_send()
        return _

    lax.fori_loop(0, groups, finish_shares, 0)
    for j in order:
        reduce_copy(j).wait_send()
        slab_copy(j).wait_send()
    for j in range(1, chips):
        spread(space, partner(j), w_send.at[j]).wait_send()
        spread(partner(j), sibling, f_send.at[j]).wait_send()
    spread(space, sibling, f_send.at[0]).wait_send()
    out.wait()


def per_device(n_space, n_snap, snapshots, eigen_vectors, singular):
    cols = snapshots.shape[1]
    rows = snapshots.shape[0] // n_snap
    snaps, rank = eigen_vectors.shape
    groups = 4
    fused = n_space == PLANE
    piece = rows // groups
    dma = pltpu.SemaphoreType.DMA
    scratch = [
        pltpu.VMEM((rows, snaps), BF16),
        pltpu.VMEM((snaps, 2 * rank), BF16),
        pltpu.VMEM((rows, rank), BF16),
        dma,
        dma((groups, n_snap)),
        dma((groups, n_snap)),
        dma,
        dma((groups,)),
    ]
    if fused:
        tall, wide = rank // 4, rank // 2
        scratch += [
            pltpu.VMEM((groups, n_space, piece, tall + wide), BF16),
            pltpu.VMEM((groups, n_space * piece, tall + wide), BF16),
            pltpu.VMEM((tall, wide), F32),
            pltpu.VMEM((n_snap, tall // n_snap, wide), F32),
            pltpu.VMEM((rank, rank), BF16),
            dma((groups, n_space)),
            dma((groups, n_space)),
            dma((groups,)),
            dma((n_snap,)),
            dma((n_snap,)),
            dma((n_snap,)),
            dma((n_snap,)),
            dma((n_space // 2,)),
            dma((n_space // 2,)),
            dma((n_space,)),
            dma,
        ]
    else:
        scratch += [pltpu.VMEM((rows, rank), BF16), pltpu.VMEM((rank, rank), F32), dma]
    anywhere = pl.BlockSpec(memory_space=pl.ANY)
    pod_modes, operator = pl.pallas_call(
        functools.partial(kernel, (n_space, n_snap, groups, fused)),
        out_shape=(
            jax.ShapeDtypeStruct((rows, rank), BF16),
            jax.ShapeDtypeStruct((rank, rank), BF16 if fused else F32),
        ),
        in_specs=[anywhere, anywhere, pl.BlockSpec(memory_space=pltpu.VMEM)],
        out_specs=(anywhere, anywhere),
        scratch_shapes=scratch,
        compiler_params=pltpu.CompilerParams(
            collective_id=0, has_side_effects=True, vmem_limit_bytes=40 * 1024 * 1024
        ),
        cost_estimate=pl.CostEstimate(
            flops=4 * rows * snaps * rank, bytes_accessed=4 * snaps * rank, transcendentals=0
        ),
    )(snapshots, eigen_vectors, singular.reshape(1, rank))
    if not fused:
        return pod_modes, lax.psum(operator, ("space", "snap"))
    return pod_modes, operator.astype(F32)


def solution(mesh):
    n_space, n_snap = mesh.shape["space"], mesh.shape["snap"]
    return jax.shard_map(
        functools.partial(per_device, n_space, n_snap),
        mesh=mesh,
        in_specs=(P("space", "snap"), P(), P()),
        out_specs=(P(("space", "snap"), None), P()),
        check_vma=False,
    )
```

time: 248 us -> 59.7 us (0.24)
  waiting for transfers between devices: 214 us -> 0 us
  Pallas kernels: 0 us -> 53.5 us
  between operations: 14.1 us -> 0.65 us
  matrix products: 5.17 us -> 0 us
  starting transfers between devices: 4.23 us -> 0 us
  other arithmetic: 3.64 us -> 1.1 us
    psum x1 -> x0, waiting for transfers between devices: 132 us -> none  [per_device(): reduced_operator = lax.psum(local_term, ('space', 'snap'))]
    reduce_scatter x1 -> x0, waiting for transfers between devices: 79.6 us -> none  [per_device(): lax.psum_scatter(jnp.concatenate([first, second], axis=1), 'snap', scatte...]
    pallas_call x0 -> x1, Pallas kernels: none -> 53.5 us  [per_device(): pl.pallas_call(functools.partial(kernel, (n_space, n_snap, groups, fused)...]
    dot_general x3 -> x0, matrix products: 5.17 us -> none  [the longest x1 2.42 us: per_device(): lax.dot_general(pod_modes, pushed, (((0,), (0,)), ((), ())), preferred_el...]
    ppermute x1 -> x0, starting transfers between devices: 4.15 us -> none  [shifted(): return lax.ppermute(block, axis, route)]
    ppermute x1 -> x0, waiting for transfers between devices: 2.83 us -> none  [shifted(): return lax.ppermute(block, axis, route)]
  transfers between devices with their start and end apart: 3 -> 0, of which waited for: 3 -> 0; matrix products, arithmetic and copies ran while one was open for 1% -> 0% of each run, Pallas kernels for 0% -> 0%
where the time goes in v1:
time: 59.7 us; the launch traced here: 59.5 us
  Pallas kernels  53.5 us (90%)
  local copies, waits for them, and re-layouts  4.19 us (7%)
  other arithmetic  1.1 us (2%)
  between operations  0.65 us (1%)
    pallas_call x1, Pallas kernels, per_device(): pl.pallas_call(functools.partial(kernel, (n_space, n_snap, groups, fused)...  53.5 us
    unnamed x7, local copies, waits for them, and re-layouts  4.19 us

profile of v1, /device:TPU:1, one launch (start us, length us, event | category | flops | bytes accessed | tf_op | source)
XLA Modules:
  0.0 59.5 jit_solution(1701544247674607359)
XLA Ops:
  0.6 0.0 copy-start
  0.6 1.6 %copy-done = bf16[2048,512]{1,0:T(8,128)(2,1)S(1)} copy-done((bf16[2048,512]{1,0:T(8,128)(2,1)S(1)}, bf16[2048,512]{1,0:T(8,128)(2,1)}, u32[]{:S(2)}) %copy-start) | copy-done | bytes 2097176
  2.2 0.0 copy-start.1
  2.2 1.2 %copy-done.1 = bf16[1024,512]{1,0:T(8,128)(2,1)S(1)} copy-done((bf16[1024,512]{1,0:T(8,128)(2,1)S(1)}, bf16[1024,512]{1,0:T(8,128)(2,1)}, u32[]{:S(2)}) %copy-start.1) | copy-done | bytes 1048600
  3.4 0.0 copy-start.2
  3.4 0.7 %copy-done.2 = f32[512]{0:T(512)S(1)} copy-done((f32[512]{0:T(512)S(1)}, f32[512]{0:T(512)}, u32[]{:S(2)}) %copy-start.2) | copy-done | bytes 2072
  4.1 53.5 %shard_map.50 = (bf16[256,512]{1,0:T(8,128)(2,1)S(1)}, bf16[512,512]{1,0:T(8,128)(2,1)S(1)}) custom-call(bf16[1024,512]{1,0:T(8,128)(2,1)S(1)} %copy-done.1, bf16[2048,512]{1,0:T(8,128)(2,1)S(1)} %copy-done, f32[1,512]{1,0:T(1,128)S(1)} %bitcast.1), custom_call_target="tpu_custom_call" | custom-call | flops 1073741824 | bytes 4194304 | tf_op jit(solution)/shard_map/pallas_call | solution.py:313
  57.7 1.1 %convert_element_type.3 = f32[512,512]{1,0:T(8,128)} convert(bf16[512,512]{1,0:T(8,128)(2,1)S(1)} %get-tuple-element.5) | non-fusion elementwise | flops 262144 | bytes 1572864 | tf_op jit(solution)/shard_map/convert_element_type | solution.py:331
  58.8 0.7 %copy.6 = bf16[256,512]{1,0:T(8,128)(2,1)} copy(bf16[256,512]{1,0:T(8,128)(2,1)S(1)} %get-tuple-element.8) | data formatting | bytes 524288
Async XLA Ops:
  0.6 1.6 %copy-start = (bf16[2048,512]{1,0:T(8,128)(2,1)S(1)}, bf16[2048,512]{1,0:T(8,128)(2,1)}, u32[]{:S(2)}) copy-start(bf16[2048,512]{1,0:T(8,128)(2,1)} %e_hbm.1) | copy-start | bytes 6291460
  2.2 1.2 %copy-start.1 = (bf16[1024,512]{1,0:T(8,128)(2,1)S(1)}, bf16[1024,512]{1,0:T(8,128)(2,1)}, u32[]{:S(2)}) copy-start(bf16[1024,512]{1,0:T(8,128)(2,1)} %x_hbm.1) | copy-start | bytes 3145732
  3.4 0.7 %copy-start.2 = (f32[512]{0:T(512)S(1)}, f32[512]{0:T(512)}, u32[]{:S(2)}) copy-start(f32[512]{0:T(512)} %param.5) | copy-start | bytes 6148

commit v2 on v1

v2 whole, which is shorter than its diff:
```python
import functools

import jax
import jax.numpy as jnp
from jax import lax
from jax.experimental import pallas as pl
from jax.experimental.pallas import tpu as pltpu
from jax.sharding import PartitionSpec as P

MESH = pl.DeviceIdType.MESH
F32, BF16 = jnp.float32, jnp.bfloat16
DEPTH = 2
PLANE = 8


def shift_vectors(vectors, snaps, rank):
    rows = 64

    def one(i, above):
        at = pl.ds(pl.multiple_of(i * rows, rows), rows)
        chunk = vectors[at, :rank].astype(F32)
        moved = pltpu.roll(chunk, 1, 0)
        first = lax.broadcasted_iota(jnp.int32, chunk.shape, 0) == 0
        vectors[at, rank:] = jnp.where(first, above, moved).astype(BF16)
        return chunk[rows - 1 :, :]

    last = vectors[snaps - 16 :, :rank].astype(F32)[15:, :]
    lax.fori_loop(0, snaps // rows, one, last)


def kernel(sizes, x_hbm, e_hbm, s_hbm, modes_hbm, op_hbm, *scratch):
    n_space, n_snap, cuts, fused = sizes
    groups = len(cuts)
    (xbuf, vectors, modes, s_ref, e_sem, x_send, x_recv, own_sem, s_sem, m_sem) = scratch[:10]
    space, snap = lax.axis_index("space"), lax.axis_index("snap")
    rows, rank = modes.shape
    cols = x_hbm.shape[1]
    snaps = cols * n_snap
    starts = [sum(cuts[:g]) for g in range(groups)]

    load_e = pltpu.make_async_copy(e_hbm, vectors.at[:, :rank], e_sem)
    load_e.start()
    load_s = pltpu.make_async_copy(s_hbm, s_ref, s_sem)
    load_s.start()
    own = pltpu.make_async_copy(
        x_hbm.at[pl.ds(pl.multiple_of(snap * rows, rows), rows), :],
        xbuf.at[snap],
        own_sem,
    )
    own.start()

    barrier = pltpu.get_barrier_semaphore()
    for j in range(1, n_snap):
        pl.semaphore_signal(
            barrier, inc=1, device_id=(space, lax.rem(snap + j, n_snap)), device_id_type=MESH
        )
    if fused:
        for j in range(1, n_space):
            pl.semaphore_signal(
                barrier, inc=1, device_id=(lax.rem(space + j, n_space), snap), device_id_type=MESH
            )
    pl.semaphore_wait(barrier, n_snap - 1 + (n_space - 1 if fused else 0))

    def block_copy(g, j):
        to = lax.rem(snap + j, n_snap)
        return pltpu.make_async_remote_copy(
            src_ref=x_hbm.at[pl.ds(pl.multiple_of(to * rows + starts[g], 16), cuts[g]), :],
            dst_ref=xbuf.at[snap, pl.ds(starts[g], cuts[g]), :],
            send_sem=x_send.at[g, j],
            recv_sem=x_recv.at[g, j],
            device_id=(space, to),
            device_id_type=MESH,
        )

    order = sorted(range(1, n_snap), key=lambda j: -min(j, n_snap - j))

    def send_blocks(g):
        for j in order:
            block_copy(g, j).start()

    depth = min(DEPTH, groups)
    for g in range(depth):
        send_blocks(g)

    load_e.wait()
    shift_vectors(vectors, snaps, rank)
    own.wait()
    load_s.wait()

    def project(g):
        at = pl.ds(starts[g], cuts[g])
        for j in order:
            block_copy(g, j).wait_send()
        if g + depth < groups:
            send_blocks(g + depth)
        for j in order:
            block_copy(g, j).wait_recv()
        sums = jnp.dot(xbuf[0, at, :], vectors[:cols, :], preferred_element_type=F32)
        for k in range(1, n_snap):
            sums += jnp.dot(
                xbuf[k, at, :], vectors[k * cols : (k + 1) * cols, :], preferred_element_type=F32
            )
        scale = s_ref[...]
        mode = (sums[:, :rank] / scale).astype(BF16)
        push = (sums[:, rank:] / scale).astype(BF16)
        modes[at, :] = mode
        pltpu.make_async_copy(modes.at[at, :], modes_hbm.at[at, :], m_sem.at[g]).start()
        return mode, push

    def finish():
        for g in range(groups):
            at = pl.ds(starts[g], cuts[g])
            pltpu.make_async_copy(modes.at[at, :], modes_hbm.at[at, :], m_sem.at[g]).wait()

    contract = (((0,), (0,)), ((), ()))
    if not fused:
        (pushed, op, op_sem) = scratch[10:]

        for g in range(groups):
            pushed[pl.ds(starts[g], cuts[g]), :] = project(g)[1]
        op[...] = lax.dot_general(modes[...], pushed[...], contract, preferred_element_type=F32)
        out = pltpu.make_async_copy(op, op_hbm, op_sem)
        out.start()
        finish()
        out.wait()
        return

    (stage, gathered, term, parts, whole, p_send, p_recv, p_own,
     r_send, r_recv, z_send, z_recv, w_send, f_send, w_recv, op_sem) = scratch[10:]
    tall, wide = rank // 4, rank // 2

    def region(g):
        start = pl.multiple_of(n_space * starts[g] + space * cuts[g], 16)
        return gathered.at[pl.ds(start, cuts[g]), :]

    def share_copy(g, j):
        to = lax.rem(space + j, n_space)
        return pltpu.make_async_remote_copy(
            src_ref=stage.at[to, pl.ds(starts[g], cuts[g]), :],
            dst_ref=region(g),
            send_sem=p_send.at[g, j],
            recv_sem=p_recv.at[g, j],
            device_id=(to, snap),
            device_id_type=MESH,
        )

    def share_own(g):
        return pltpu.make_async_copy(
            stage.at[space, pl.ds(starts[g], cuts[g]), :], region(g), p_own.at[g]
        )

    def add_term(g):
        share_own(g).wait()
        for j in range(1, n_space):
            share_copy(g, j).wait_recv()
        at = pl.ds(n_space * starts[g], n_space * cuts[g])
        return lax.dot_general(
            gathered[at, :tall], gathered[at, tall:], contract, preferred_element_type=F32
        )

    for g in range(groups):
        mode, push = project(g)
        at = pl.ds(starts[g], cuts[g])
        for p in range(n_space):
            stage[p, at, :tall] = mode[:, (p // 2) * tall : (p // 2 + 1) * tall]
            stage[p, at, tall:] = push[:, (p % 2) * wide : (p % 2 + 1) * wide]
        for j in (3, 4, 5, 2, 6, 1, 7):
            share_copy(g, j).start()
        share_own(g).start()
        if g == 1:
            term[...] = add_term(0)
        elif g > 1:
            term[...] += add_term(g - 1)
    term[...] += add_term(groups - 1)

    slab = tall // n_snap

    def reduce_copy(j):
        to = lax.rem(snap + j, n_snap)
        return pltpu.make_async_remote_copy(
            src_ref=term.at[pl.ds(pl.multiple_of(to * slab, slab), slab), :],
            dst_ref=parts.at[j],
            send_sem=r_send.at[j],
            recv_sem=r_recv.at[j],
            device_id=(space, to),
            device_id_type=MESH,
        )

    for j in order:
        reduce_copy(j).start()
    mine = pl.multiple_of(snap * slab, slab)
    total = term[pl.ds(mine, slab), :]
    for j in order:
        reduce_copy(j).wait_recv()
    for j in order:
        total = total + parts[j]

    def place(p, start, size):
        return whole.at[
            pl.ds(pl.multiple_of((p // 2) * tall + start, size), size),
            pl.ds(pl.multiple_of(lax.rem(p, 2) * wide, wide), wide),
        ]

    parts[0] = total
    piece_at = place(space, mine, slab)
    piece_at[...] = parts[0].astype(BF16)

    def slab_copy(j):
        return pltpu.make_async_remote_copy(
            src_ref=piece_at,
            dst_ref=piece_at,
            send_sem=z_send.at[j],
            recv_sem=z_recv.at[j],
            device_id=(space, lax.rem(snap + j, n_snap)),
            device_id_type=MESH,
        )

    def slab_arrival(j):
        origin = lax.rem(snap + n_snap - j, n_snap)
        at = place(space, origin * slab, slab)
        return pltpu.make_async_remote_copy(
            src_ref=at, dst_ref=at, send_sem=z_send.at[j], recv_sem=z_recv.at[j],
            device_id=(space, lax.rem(snap + j, n_snap)), device_id_type=MESH,
        )

    chip, core = space // 2, lax.rem(space, 2)
    chips = n_space // 2
    sibling = space + 1 - 2 * core
    near = sorted(range(n_snap), key=lambda j: min(j, n_snap - j))

    def partner(i):
        return lax.rem(chip + i, chips) * 2 + core

    def spread(i, j, p, to):
        at = place(p, lax.rem(snap + n_snap - j, n_snap) * slab, slab)
        return pltpu.make_async_remote_copy(
            src_ref=at, dst_ref=at, send_sem=w_send.at[i, j], recv_sem=w_recv.at[p, j],
            device_id=(to, snap), device_id_type=MESH,
        )

    def hand_over(i, j):
        at = place(partner(i), lax.rem(snap + n_snap - j, n_snap) * slab, slab)
        return pltpu.make_async_remote_copy(
            src_ref=at, dst_ref=at, send_sem=f_send.at[i, j], recv_sem=w_recv.at[partner(i), j],
            device_id=(sibling, snap), device_id_type=MESH,
        )

    for j in order:
        slab_copy(j).start()
    for j in near:
        if j:
            slab_arrival(j).wait_recv()
        for i in (2, 1, 3):
            spread(i, j, space, partner(i)).start()
        hand_over(0, j).start()
    for j in near:
        for i in (1, 3, 2):
            hand_over(i, j).wait_recv()
            hand_over(i, j).start()
    for j in near:
        for i in range(chips):
            there = lax.rem(chip + i, chips) * 2 + 1 - core
            spread(i, j, there, sibling).wait_recv()
    out = pltpu.make_async_copy(whole, op_hbm, op_sem)
    out.start()

    finish()

    for g in range(groups):
        for j in range(1, n_space):
            share_copy(g, j).wait_send()
    for j in order:
        reduce_copy(j).wait_send()
        slab_copy(j).wait_send()
    for j in near:
        for i in range(chips):
            if i:
                spread(i, j, space, partner(i)).wait_send()
            hand_over(i, j).wait_send()
    out.wait()


def cut(rows):
    if rows % 256 == 0:
        return [share * rows // 16 for share in (5, 5, 4, 2)]
    return [rows // 4] * 4 if rows % 64 == 0 else [rows]


def per_device(n_space, n_snap, snapshots, eigen_vectors, singular):
    cols = snapshots.shape[1]
    rows = snapshots.shape[0] // n_snap
    snaps, rank = eigen_vectors.shape
    fused = n_space == PLANE
    cuts = cut(rows)
    groups = len(cuts)
    dma = pltpu.SemaphoreType.DMA
    scratch = [
        pltpu.VMEM((n_snap, rows, snaps // n_snap), BF16),
        pltpu.VMEM((snaps, 2 * rank), BF16),
        pltpu.VMEM((rows, rank), BF16),
        pltpu.VMEM((1, rank), F32),
        dma,
        dma((groups, n_snap)),
        dma((groups, n_snap)),
        dma,
        dma,
        dma((groups,)),
    ]
    if fused:
        tall, wide = rank // 4, rank // 2
        scratch += [
            pltpu.VMEM((n_space, rows, tall + wide), BF16),
            pltpu.VMEM((n_space * rows, tall + wide), BF16),
            pltpu.VMEM((tall, wide), F32),
            pltpu.VMEM((n_snap, tall // n_snap, wide), F32),
            pltpu.VMEM((rank, rank), BF16),
            dma((groups, n_space)),
            dma((groups, n_space)),
            dma((groups,)),
            dma((n_snap,)),
            dma((n_snap,)),
            dma((n_snap,)),
            dma((n_snap,)),
            dma((n_space // 2, n_snap)),
            dma((n_space // 2, n_snap)),
            dma((n_space, n_snap)),
            dma,
        ]
    else:
        scratch += [pltpu.VMEM((rows, rank), BF16), pltpu.VMEM((rank, rank), F32), dma]
    operands = (snapshots, eigen_vectors, singular.reshape(1, rank))
    in_hbm = pl.BlockSpec(memory_space=pltpu.HBM)
    pod_modes, operator = pl.pallas_call(
        functools.partial(kernel, (n_space, n_snap, cuts, fused)),
        out_shape=(
            jax.ShapeDtypeStruct((rows, rank), BF16),
            jax.ShapeDtypeStruct((rank, rank), BF16 if fused else F32),
        ),
        in_specs=[in_hbm] * 3,
        out_specs=(in_hbm, in_hbm),
        scratch_shapes=scratch,
        compiler_params=pltpu.CompilerParams(
            collective_id=0, has_side_effects=True, vmem_limit_bytes=40 * 1024 * 1024
        ),
        cost_estimate=pl.CostEstimate(
            flops=4 * rows * snaps * rank, bytes_accessed=4 * snaps * rank, transcendentals=0
        ),
    )(*[pltpu.with_memory_space_constraint(a, pltpu.HBM) for a in operands])
    if not fused:
        return pod_modes, lax.psum(operator, ("space", "snap"))
    return pod_modes, operator.astype(F32)


def solution(mesh):
    n_space, n_snap = mesh.shape["space"], mesh.shape["snap"]
    return jax.shard_map(
        functools.partial(per_device, n_space, n_snap),
        mesh=mesh,
        in_specs=(P("space", "snap"), P(), P()),
        out_specs=(P(("space", "snap"), None), P()),
        check_vma=False,
    )
```

time: 59.7 us -> 56.5 us (0.946)
  local copies, waits for them, and re-layouts: 4.19 us -> 0.7 us
    unnamed x7 -> x1, local copies, waits for them, and re-layouts: 4.19 us -> 0.7 us
where the time goes in v2:
time: 56.5 us; the launch traced here: 56.4 us
  Pallas kernels  53.9 us (95%)
  other arithmetic  1.1 us (2%)
  local copies, waits for them, and re-layouts  0.7 us (1%)
  between operations  0.64 us (1%)
    pallas_call x1, Pallas kernels, per_device(): pl.pallas_call(functools.partial(kernel, (n_space, n_snap, cuts, fused)),...  53.9 us

profile of v2, /device:TPU:1, one launch (start us, length us, event | category | flops | bytes accessed | tf_op | source)
XLA Modules:
  0.0 56.4 jit_solution(15256300371383758581)
XLA Ops:
  0.6 53.9 %shard_map.50 = (bf16[256,512]{1,0:T(8,128)(2,1)S(1)}, bf16[512,512]{1,0:T(8,128)(2,1)S(1)}) custom-call(bf16[1024,512]{1,0:T(8,128)(2,1)} %x_hbm.1, bf16[2048,512]{1,0:T(8,128)(2,1)} %e_hbm.1, f32[1,512]{1,0:T(1,128)} %bitcast.1), custom_call_target="tpu_custom_call" | custom-call | flops 1073741824 | bytes 4194304 | tf_op jit(solution)/shard_map/pallas_call | solution.py:333
  54.5 1.1 %convert_element_type.3 = f32[512,512]{1,0:T(8,128)} convert(bf16[512,512]{1,0:T(8,128)(2,1)S(1)} %get-tuple-element.5) | non-fusion elementwise | flops 262144 | bytes 1572864 | tf_op jit(solution)/shard_map/convert_element_type | solution.py:351
  55.6 0.7 %copy.6 = bf16[256,512]{1,0:T(8,128)(2,1)} copy(bf16[256,512]{1,0:T(8,128)(2,1)S(1)} %get-tuple-element.8) | data formatting | bytes 524288

commit v3 on v2

--- a/solution.py
+++ b/solution.py
@@ -282,7 +282,7 @@
 
 def cut(rows):
     if rows % 256 == 0:
-        return [share * rows // 16 for share in (5, 5, 4, 2)]
+        return [share * rows // 16 for share in (2, 4, 4, 4, 2)]
     return [rows // 4] * 4 if rows % 64 == 0 else [rows]
 
 

time: 56.5 us -> 56 us (level)
  no operation moved by 1% of the time
where the time goes in v3:
time: 56 us; the launch traced here: 55.9 us
  Pallas kernels  53.4 us (95%)
  other arithmetic  1.1 us (2%)
  local copies, waits for them, and re-layouts  0.7 us (1%)
  between operations  0.64 us (1%)
    pallas_call x1, Pallas kernels, per_device(): pl.pallas_call(functools.partial(kernel, (n_space, n_snap, cuts, fused)),...  53.4 us

profile of v3, /device:TPU:1, one launch (start us, length us, event | category | flops | bytes accessed | tf_op | source)
XLA Modules:
  0.0 55.9 jit_solution(10333765847973320799)
XLA Ops:
  0.6 53.4 %shard_map.50 = (bf16[256,512]{1,0:T(8,128)(2,1)S(1)}, bf16[512,512]{1,0:T(8,128)(2,1)S(1)}) custom-call(bf16[1024,512]{1,0:T(8,128)(2,1)} %x_hbm.1, bf16[2048,512]{1,0:T(8,128)(2,1)} %e_hbm.1, f32[1,512]{1,0:T(1,128)} %bitcast.1), custom_call_target="tpu_custom_call" | custom-call | flops 1073741824 | bytes 4194304 | tf_op jit(solution)/shard_map/pallas_call | solution.py:333
  54.1 1.1 %convert_element_type.3 = f32[512,512]{1,0:T(8,128)} convert(bf16[512,512]{1,0:T(8,128)(2,1)S(1)} %get-tuple-element.5) | non-fusion elementwise | flops 262144 | bytes 1572864 | tf_op jit(solution)/shard_map/convert_element_type | solution.py:351
  55.2 0.7 %copy.6 = bf16[256,512]{1,0:T(8,128)(2,1)} copy(bf16[256,512]{1,0:T(8,128)(2,1)S(1)} %get-tuple-element.8) | data formatting | bytes 524288
